TPU v7x, 1024 devices: a whole 4x8x16 slice. The times are simulated.
1024 devices in a mesh: expert: 32 (over y, x), tensor: 32 (over z, core).
Axes of the slice: x: 4, y: 8, z: 16, core: 2. Of those that a mesh axis runs over, the one named last changes fastest.
Arguments:
- hidden_in: bfloat16 [4096, 4096], P('expert'), may hold values from -6 to 6
- w_latent: bfloat16 [4096, 1024], P(None, 'tensor'), may hold values from -0.09375 to 0.09375
- routes: int32 [4096, 22], P('expert'), may hold values from 0 to 255, all different within a row; in each aligned block of 128 rows (0 to 127, 128 to 255, ...) at most 16 rows name the same one
- gates: float32 [4096, 22], P('expert'), may hold values from 0.05 to 1
- expert_gate: bfloat16 [1024, 1024, 336], P(('expert', 'tensor')), may hold values from -0.1875 to 0.1875
- expert_up: bfloat16 [1024, 1024, 336], P(('expert', 'tensor')), may hold values from -0.1875 to 0.1875
- expert_down: bfloat16 [1024, 336, 1024], P(('expert', 'tensor')), may hold values from -0.15625 to 0.15625
- shared_gate: bfloat16 [4096, 2688], P(None, 'tensor'), may hold values from -0.09375 to 0.09375
- shared_up: bfloat16 [4096, 2688], P(None, 'tensor'), may hold values from -0.09375 to 0.09375
- shared_down: bfloat16 [2688, 4096], P('tensor'), may hold values from -0.125 to 0.125
- w_restore: bfloat16 [1024, 4096], P('tensor'), may hold values from -0.1875 to 0.1875
Outputs:
- mixed: bfloat16 [4096, 4096], P(('expert', 'tensor'))
Inputs may be any that keep to these rules, and one draw needn't show every extreme that they name: `routes`: each row names 22 different experts; among the 128 rows of one index of expert (aligned blocks), no expert is named more than 16 times.
All inputs are finite; a program needn't handle non-finite values.
Results may differ from a plain program's by a relative error of at most 0.03.
Values may be sent and summed in bfloat16 or wider, within the bound.
No kernel may reach another device: no remote copies, remote signals or barrier semaphores. Data moves between devices by JAX's collectives and lax.ppermute only.
A program may use at most 32 MiB of HBM per device.

v0:
```python
import jax
import jax.numpy as jnp
from jax import lax
from jax.sharding import PartitionSpec as P


def shards(
    hidden_in,
    w_latent,
    routes,
    gates,
    expert_gate,
    expert_up,
    expert_down,
    shared_gate,
    shared_up,
    shared_down,
    w_restore,
):
    groups = lax.axis_size("expert")
    tensor_size = lax.axis_size("tensor")
    position = lax.axis_index("tensor")
    row_count = hidden_in.shape[0]
    top_count = routes.shape[1]
    width = w_restore.shape[0] * tensor_size
    experts = groups * tensor_size // 4
    capacity = 4 * max(1, 3 * row_count * top_count // (8 * experts))
    latent_cols = jnp.dot(hidden_in, w_latent, preferred_element_type=jnp.float32).astype(
        jnp.bfloat16
    )
    latent = lax.all_gather(latent_cols, "tensor", axis=1, tiled=True)
    targets = jnp.arange(groups, dtype=jnp.int32) * (tensor_size // 4) + position // 4
    matched = routes[:, :, None] == targets[None, None, :]
    hit_count = jnp.sum(matched.astype(jnp.bfloat16), axis=1)
    weight = jnp.sum(jnp.where(matched, gates[:, :, None], 0.0), axis=1)
    below_mask = (
        lax.broadcasted_iota(jnp.int32, (row_count, row_count), 0)
        > lax.broadcasted_iota(jnp.int32, (row_count, row_count), 1)
    ).astype(jnp.bfloat16)
    earlier = jnp.dot(below_mask, hit_count, preferred_element_type=jnp.float32)
    slot_ids = jnp.arange(capacity, dtype=jnp.float32)
    slot_mask = (hit_count.T[:, None, :] > 0.5) & (
        jnp.abs(earlier.T[:, None, :] - slot_ids[None, :, None]) < 0.5
    )
    row_iota = jnp.arange(row_count, dtype=jnp.int32)
    filled = jnp.any(slot_mask, axis=-1)
    row_index = jnp.sum(jnp.where(slot_mask, row_iota[None, None, :], 0), axis=-1) + jnp.where(
        filled, 0, row_count
    )
    padded_latent = jnp.concatenate([latent, jnp.zeros((1, width), jnp.bfloat16)], axis=0)
    outbound = padded_latent[row_index]
    block = lax.all_to_all(outbound, "expert", split_axis=0, concat_axis=0, tiled=True)
    flat_rows = block.reshape(-1, block.shape[-1])
    gate_act = jnp.dot(flat_rows, expert_gate[0], preferred_element_type=jnp.float32)
    up_act = jnp.dot(flat_rows, expert_up[0], preferred_element_type=jnp.float32)
    hidden_act = (jax.nn.silu(gate_act) * up_act).astype(jnp.bfloat16)
    result = jnp.dot(hidden_act, expert_down[0], preferred_element_type=jnp.float32).astype(
        jnp.bfloat16
    )
    expert_out = result.reshape(block.shape[0], block.shape[1], result.shape[-1])
    returned = lax.all_to_all(expert_out, "expert", split_axis=0, concat_axis=0, tiled=True)
    padded_weight = jnp.concatenate([weight, jnp.zeros((1, groups), jnp.float32)], axis=0)
    group_iota = jnp.arange(groups, dtype=jnp.int32)
    gate_slot = padded_weight[row_index, group_iota[:, None]]
    scaled = returned.astype(jnp.float32) * gate_slot[:, :, None]
    routed_terms = (
        jnp.zeros((row_count + 1, width), jnp.float32)
        .at[row_index.reshape(-1)]
        .add(scaled.reshape(-1, width))[:row_count]
    )
    routed = lax.psum_scatter(routed_terms, "tensor", scatter_dimension=1, tiled=True).astype(
        jnp.bfloat16
    )
    shared_gate_act = jnp.dot(hidden_in, shared_gate, preferred_element_type=jnp.float32)
    shared_up_act = jnp.dot(hidden_in, shared_up, preferred_element_type=jnp.float32)
    shared_hidden = (jax.nn.silu(shared_gate_act) * shared_up_act).astype(jnp.bfloat16)
    return lax.psum_scatter(
        (
            jnp.dot(shared_hidden, shared_down, preferred_element_type=jnp.float32)
            + jnp.dot(routed, w_restore, preferred_element_type=jnp.float32)
        ).astype(jnp.bfloat16),
        "tensor",
        scatter_dimension=0,
        tiled=True,
    )


def solution(mesh):
    in_specs = (
        P("expert", None),
        P(None, "tensor"),
        P("expert", None),
        P("expert", None),
        P(("expert", "tensor"), None, None),
        P(("expert", "tensor"), None, None),
        P(("expert", "tensor"), None, None),
        P(None, "tensor"),
        P(None, "tensor"),
        P("tensor", None),
        P("tensor", None),
    )
    out_specs = P(("expert", "tensor"), None)
    return jax.shard_map(shards, mesh=mesh, in_specs=in_specs, out_specs=out_specs, check_vma=False)
```

profile of v0, /device:TPU:1, one launch (start us, length us, event | category | flops | bytes accessed | tf_op | source)
XLA Modules:
  0.0 467.4 jit_solution(10621004474037789417)
XLA Ops:
  6.5 0.9 fusion.19
  7.5 0.1 fusion.21
  7.6 0.6 select_reduce_fusion
  8.2 0.6 fusion.20
  8.9 0.1 reshape.90
  9.0 1.4 convolution_convert_fusion.1
  10.4 45.1 %all_gather.3 = bf16[128,1024]{0,1:T(8,128)(2,1)S(1)} all-gather(bf16[128,32]{0,1:T(8,128)(2,1)S(1)} %convolution_convert_fusion.1), channel_id=1, replica_groups=mesh['expert'=32,'tensor'=32] {'tensor'}, dimensions={1}, use_global_device_ids=true | all-gather | bytes 270336 | tf_op jit(solution)/shard_map/all_gather | solution.py:31
  55.5 0.1 copy.28
  55.7 2.1 gather_fusion
  57.8 36.7 %all_to_all.10 = bf16[32,16,1024]{2,1,0:T(8,128)(2,1)S(1)} all-to-all(bf16[32,16,1024]{2,1,0:T(8,128)(2,1)S(1)} %bitcast.40), channel_id=1, replica_groups=mesh['expert'=32,'tensor'=32] {'expert'}, dimensions={0} | all-to-all | bytes 2097152 | tf_op jit(solution)/shard_map/all_to_all | solution.py:52
  94.5 0.6 fusion.7
  95.0 0.5 copy-done.6
  95.6 3.4 convolution_convert_fusion
  98.9 6.0 %all-to-all-start.1 = ((bf16[32,16,1024]{2,1,0:T(8,128)(2,1)}), bf16[32,16,1024]{2,1,0:T(8,128)(2,1)S(1)}, u32[]{:S(2)}, u32[]{:S(2)}) async-start(bf16[32,16,1024]{2,1,0:T(8,128)(2,1)} %bitcast.8), calls=%async_computation.1 | async-start | bytes 2097152 | tf_op jit(solution)/shard_map/all_to_all | solution.py:61
  105.0 0.1 add.86
  105.1 0.1 reshape.96
  105.2 0.1 fusion.14
  105.3 0.1 copy.25
  105.4 3.8 gather_fusion.1
  109.2 0.1 reshape.99
  109.3 21.3 %all-to-all-done.1 = bf16[32,16,1024]{2,1,0:T(8,128)(2,1)S(1)} async-done(((bf16[32,16,1024]{2,1,0:T(8,128)(2,1)}), bf16[32,16,1024]{2,1,0:T(8,128)(2,1)S(1)}, u32[]{:S(2)}, u32[]{:S(2)}) %all-to-all-start.1) | async-done | bytes 1048608 | tf_op jit(solution)/shard_map/all_to_all | solution.py:61
  130.6 1.6 convert_multiply_fusion
  132.2 5.9 %scatter_custom_fusion = f32[129,1024]{1,0:T(8,128)S(1)} fusion(s32[512]{0:T(512)S(1)} %bitcast.46, f32[512,1024]{1,0:T(8,128)} %bitcast.43, f32[]{:T(128)} %constant.16.clone.1), kind=kCustom, calls=%fused_computation.26 | custom fusion | flops 524288 | bytes 528896 | tf_op jit(solution)/shard_map/scatter-add | solution.py:69
  138.1 1.0 copy.26
  139.2 0.5 fusion.31
  139.7 2.8 fusion.3
  142.4 96.8 %reduce-scatter.4.cloned.1.call-done = f32[32,128]{1,0:T(8,128)} async-done(((f32[1024,128]{1,0:T(8,128)}), f32[32,128]{1,0:T(8,128)}) %reduce-scatter.4.cloned.1.call-update) | async-done | bytes 16400
  239.3 0.8 copy.27
  240.1 1.5 fusion
  241.6 1.3 dynamic-slice
  243.5 215.6 %all-reduce.5.cloned.1.call-done = bf16[128,4096]{1,0:T(8,128)(2,1)} async-done(((bf16[128,4096]{1,0:T(8,128)(2,1)}), bf16[128,4096]{1,0:T(8,128)(2,1)}) %all-reduce.5.cloned.1.call-update) | async-done | bytes 1048592
  459.1 1.5 constant_dynamic-slice_fusion
  (26 shorter events, 0.3 us)
Async XLA Ops:
  6.5 2.5 copy-start
  57.8 36.7 %copy-start.2 = (bf16[1,1024,336]{1,2,0:T(8,128)(2,1)S(1)}, bf16[1,1024,336]{1,2,0:T(8,128)(2,1)}, u32[]{:S(2)}) copy-start(bf16[1,1024,336]{1,2,0:T(8,128)(2,1)} %param.15) | copy-start | bytes 2064388
  94.5 1.1 copy-start.6
  98.9 6.2 %copy-start.4 = (s32[128,22]{0,1:T(8,128)S(1)}, s32[128,22]{0,1:T(8,128)}, u32[]{:S(2)}) copy-start(s32[128,22]{0,1:T(8,128)} %param.13) | copy-start | bytes 33796
  98.9 6.2 %copy-start.5 = (f32[128,22]{0,1:T(8,128)S(1)}, f32[128,22]{0,1:T(8,128)}, u32[]{:S(2)}) copy-start(f32[128,22]{0,1:T(8,128)} %param.14) | copy-start | bytes 33796
  98.9 31.7 %all-to-all-start.1 = ((bf16[32,16,1024]{2,1,0:T(8,128)(2,1)}), bf16[32,16,1024]{2,1,0:T(8,128)(2,1)S(1)}, u32[]{:S(2)}, u32[]{:S(2)}) async-start(bf16[32,16,1024]{2,1,0:T(8,128)(2,1)} %bitcast.8), calls=%async_computation.1 | async-start | bytes 2097152 | tf_op jit(solution)/shard_map/all_to_all | solution.py:61
  105.0 134.3 %reduce-scatter.4.cloned.1.call-start = ((), (), s32[]{:S(2)}) async-start(), calls=%async_computation.3 | async-start | bytes 540672
  132.2 7.0 %copy-start.1 = (bf16[4096,84]{0,1:T(8,128)(2,1)S(1)}, bf16[4096,84]{0,1:T(8,128)(2,1)}, u32[]{:S(2)}) copy-start(bf16[4096,84]{0,1:T(8,128)(2,1)} %param.18) | copy-start | bytes 2064388
  139.1 320.0 %all-reduce.5.cloned.1.call-start = ((), (), s32[]{:S(2)}) async-start(), calls=%async_computation.4 | async-start | bytes 2097152
  139.7 100.4 %copy-start.3 = (bf16[32,4096]{1,0:T(8,128)(2,1)S(1)}, bf16[32,4096]{1,0:T(8,128)(2,1)}, u32[]{:S(2)}) copy-start(bf16[32,4096]{1,0:T(8,128)(2,1)} %param.21) | copy-start | bytes 786436
Sparse Core Ops, SparseCore 0:
  139.3 99.9 reduce-scatter.3
  241.7 217.3 all-reduce.4
where the time goes:
time: 468 us; the launch traced here: 467 us
  waiting for transfers between devices  334 us (71%)
  blocking collectives  81.8 us (17%)
  between operations  14.2 us (3%)
  local copies, waits for them, and re-layouts  11.6 us (2%)
  matrix products  10.2 us (2%)
  other arithmetic  9.8 us (2%)
  starting transfers between devices  6.11 us (1%)
    unnamed x4, waiting for transfers between devices  312 us
    all_gather x1, blocking collectives, shards(): latent = lax.all_gather(latent_cols, 'tensor', axis=1, tiled=True)  45.1 us
    all_to_all x1, blocking collectives, shards(): lax.all_to_all(outbound, 'expert', split_axis=0, concat_axis=0, tiled=True)  36.7 us
    all_to_all x1, waiting for transfers between devices, shards(): lax.all_to_all(expert_out, 'expert', split_axis=0, concat_axis=0, tiled=T...  21.3 us
  transfers between devices with their start and end apart: 3, of which 3 were waited for; matrix products, arithmetic and copies ran while one was open for 2% of the time, Pallas kernels for 0%

commit v1 on v0

v1 whole, which is shorter than its diff:
```python
import jax
import jax.numpy as jnp
from jax import lax
from jax.sharding import Mesh, PartitionSpec as P

TENSOR = ("z", "c")
BF16 = jnp.bfloat16
F32 = jnp.float32


def dot(a, b):
    return jnp.dot(a, b, preferred_element_type=F32)


def swap_cores(value):
    return lax.ppermute(value, "c", [(0, 1), (1, 0)])


def shards(
    hidden_in,
    w_latent,
    routes,
    gates,
    expert_gate,
    expert_up,
    expert_down,
    shared_gate,
    shared_up,
    shared_down,
    w_restore,
):
    groups = lax.axis_size("expert")
    chips = lax.axis_size("z")
    cores = lax.axis_size("c")
    tensor_size = chips * cores
    core = lax.axis_index("c")
    position = lax.axis_index("z") * cores + core
    rows = hidden_in.shape[0]
    block = w_restore.shape[0]
    width = block * tensor_size
    model = hidden_in.shape[1]
    top = routes.shape[1]
    experts = groups * tensor_size // 4
    capacity = 4 * max(1, 3 * rows * top // (8 * experts))

    latent_cols = dot(hidden_in, w_latent).astype(BF16)
    copies = jnp.broadcast_to(latent_cols.T[None], (tensor_size, block, rows))
    latent_t = lax.all_to_all(copies, TENSOR, 0, 0, tiled=True).reshape(width, rows)

    targets = jnp.arange(groups, dtype=jnp.int32) * (tensor_size // 4) + position // 4
    matched = routes[:, :, None] == targets[None, None, :]
    hits = jnp.sum(matched.astype(BF16), axis=1)
    weight = jnp.sum(jnp.where(matched, gates[:, :, None], 0.0), axis=1)
    below = (
        lax.broadcasted_iota(jnp.int32, (rows, rows), 0)
        > lax.broadcasted_iota(jnp.int32, (rows, rows), 1)
    ).astype(BF16)
    earlier = dot(below, hits)
    slots = jnp.where(hits > 0.5, earlier, -1.0).T
    slot_ids = jnp.arange(capacity, dtype=F32)
    slot_mask = slots[:, None, :] == slot_ids[None, :, None]
    pick = slot_mask.astype(BF16).reshape(groups * capacity, rows)
    weighted = jnp.where(slot_mask, weight.T[:, None, :], 0.0).reshape(groups * capacity, rows)
    weighted_high = weighted.astype(BF16)
    weighted_low = (weighted - weighted_high.astype(F32)).astype(BF16)

    outbound = lax.dot_general(
        pick, latent_t, (((1,), (1,)), ((), ())), preferred_element_type=F32
    ).astype(BF16)
    taken = lax.all_to_all(
        outbound.reshape(groups, capacity, width), "expert", 0, 0, tiled=True
    ).reshape(groups * capacity, width)
    gate_act = dot(taken, expert_gate[0])
    up_act = dot(taken, expert_up[0])
    act = (jax.nn.silu(gate_act) * up_act).astype(BF16)
    part = dot(act, expert_down[0]).astype(BF16)
    returned = lax.all_to_all(
        part.reshape(groups, capacity, width), "expert", 0, 0, tiled=True
    ).reshape(groups * capacity, width)

    def combine(w):
        return lax.dot_general(
            returned, w, (((0,), (0,)), ((), ())), preferred_element_type=F32
        )

    routed_terms = (combine(weighted_high) + combine(weighted_low)).astype(BF16)
    pieces = lax.all_to_all(
        routed_terms.reshape(tensor_size, block, rows), TENSOR, 0, 0, tiled=True
    )
    routed_t = jnp.sum(pieces.astype(F32), axis=0).astype(BF16)

    shared_act = (jax.nn.silu(dot(hidden_in, shared_gate)) * dot(hidden_in, shared_up)).astype(BF16)
    total = dot(shared_act, shared_down) + lax.dot_general(
        routed_t, w_restore, (((0,), (0,)), ((), ())), preferred_element_type=F32
    )
    own = rows // tensor_size
    by_core = total.reshape(chips, cores, own, model)
    keep = jnp.where(core == 0, by_core[:, 0], by_core[:, 1])
    give = jnp.where(core == 0, by_core[:, 1], by_core[:, 0]).astype(BF16)
    pair = (keep + swap_cores(give).astype(F32)).astype(BF16)
    final = lax.all_to_all(pair, "z", 0, 0, tiled=True)
    return jnp.sum(final.astype(F32), axis=0).astype(BF16)


def solution(mesh):
    shape = mesh.devices.shape
    split = Mesh(mesh.devices.reshape(shape[0], shape[1] // 2, 2), ("expert", "z", "c"))
    both = ("expert", "z", "c")
    in_specs = (
        P("expert", None),
        P(None, TENSOR),
        P("expert", None),
        P("expert", None),
        P(both, None, None),
        P(both, None, None),
        P(both, None, None),
        P(None, TENSOR),
        P(None, TENSOR),
        P(TENSOR, None),
        P(TENSOR, None),
    )
    return jax.shard_map(
        shards, mesh=split, in_specs=in_specs, out_specs=P(both, None), check_vma=False
    )
```

time: 468 us -> 191 us (0.41)
  the two profiles are of different devices: /device:TPU:1 before, /device:TPU:66 now
where the time goes in v1:
time: 191 us
  blocking collectives  72 us (38%)
  waiting for transfers between devices  66.8 us (35%)
  starting transfers between devices  32.3 us (17%)
  matrix products  13.7 us (7%)
  local copies, waits for them, and re-layouts  3.85 us (2%)
    all_to_all x1, blocking collectives, shards(): lax.all_to_all(outbound.reshape(groups, capacity, width), 'expert', 0, 0,...  37.6 us
    all_to_all x1, blocking collectives, shards(): final = lax.all_to_all(pair, 'z', 0, 0, tiled=True)  34.4 us
    all_to_all x1, waiting for transfers between devices, shards(): lax.all_to_all(part.reshape(groups, capacity, width), 'expert', 0, 0, til...  26.6 us
    all_to_all x1, waiting for transfers between devices, shards(): lax.all_to_all(copies, TENSOR, 0, 0, tiled=True).reshape(width, rows)  20.6 us
    all_to_all x1, starting transfers between devices, shards(): lax.all_to_all(copies, TENSOR, 0, 0, tiled=True).reshape(width, rows)  18.7 us
    all_to_all x1, waiting for transfers between devices, shards(): lax.all_to_all(routed_terms.reshape(tensor_size, block, rows), TENSOR, 0,...  17.8 us
    dot_general x6, matrix products, dot(): return jnp.dot(a, b, preferred_element_type=F32)  8.85 us
    all_to_all x1, starting transfers between devices, shards(): lax.all_to_all(routed_terms.reshape(tensor_size, block, rows), TENSOR, 0,...  5.94 us
  transfers between devices with their start and end apart: 4, of which 4 were waited for; matrix products, arithmetic and copies ran while one was open for 2% of the time, Pallas kernels for 0%

profile of v1, /device:TPU:66, one launch (start us, length us, event | category | flops | bytes accessed | tf_op | source)
XLA Modules:
  0.0 190.7 jit_solution(5699276051430450661)
XLA Ops:
  0.0 0.0 copy-start
  0.0 1.2 copy-done
  1.2 1.4 convolution_convert_fusion.2
  2.6 0.8 broadcast_in_dim.41
  3.4 18.7 %all-to-all-start = ((bf16[32,32,128]{2,1,0:T(8,128)(2,1)}), bf16[32,32,128]{2,1,0:T(8,128)(2,1)S(1)}, u32[]{:S(2)}, u32[]{:S(2)}) async-start(bf16[32,32,128]{2,1,0:T(8,128)(2,1)} %broadcast_in_dim.41), calls=%async_computation | async-start | bytes 524288 | tf_op jit(solution)/shard_map/all_to_all | solution.py:48
  22.1 0.1 fusion.22
  22.2 0.1 convolution_select_fusion
  22.4 0.1 iota_compare_fusion
  22.4 20.6 %all-to-all-done = bf16[32,32,128]{2,1,0:T(8,128)(2,1)S(1)} async-done(((bf16[32,32,128]{2,1,0:T(8,128)(2,1)}), bf16[32,32,128]{2,1,0:T(8,128)(2,1)S(1)}, u32[]{:S(2)}, u32[]{:S(2)}) %all-to-all-start) | async-done | bytes 262176 | tf_op jit(solution)/shard_map/all_to_all | solution.py:48
  43.0 0.4 convolution_convert_fusion.1
  43.5 37.6 %all_to_all.25 = bf16[32,16,1024]{2,1,0:T(8,128)(2,1)S(1)} all-to-all(bf16[32,16,1024]{2,1,0:T(8,128)(2,1)S(1)} %bitcast.69), channel_id=1, replica_groups=mesh['expert'=32,'z'=16,'c'=2] {'expert'}, dimensions={0} | all-to-all | bytes 2097152 | tf_op jit(solution)/shard_map/all_to_all | solution.py:70
  81.1 0.6 fusion.11
  81.6 3.6 %convolution_convert_fusion = bf16[512,1024]{1,0:T(8,128)(2,1)} fusion(bf16[512,1024]{1,0:T(8,128)(2,1)S(1)} %bitcast.68, bf16[1,336,1024]{2,1,0:T(8,128)(2,1)} %param.17, bf16[1,1024,336]{1,2,0:T(8,128)(2,1)} %param.16, f32[512,336]{0,1:T(8,128)S(1)} %fusion.11), kind=kOutput, calls=%fused_computation.1 | convolution fusion | flops 706199552 | bytes 4161536 | tf_op jit(solution)/shard_map/dot_general | solution.py:12
  85.2 5.7 %all-to-all-start.2 = ((bf16[32,16,1024]{2,1,0:T(8,128)(2,1)}), bf16[32,16,1024]{2,1,0:T(8,128)(2,1)S(1)}, u32[]{:S(2)}, u32[]{:S(2)}) async-start(bf16[32,16,1024]{2,1,0:T(8,128)(2,1)} %bitcast.8), calls=%async_computation.2 | async-start | bytes 2097152 | tf_op jit(solution)/shard_map/all_to_all | solution.py:77
  90.9 0.1 fusion.19
  91.0 26.6 %all-to-all-done.2 = bf16[32,16,1024]{2,1,0:T(8,128)(2,1)S(1)} async-done(((bf16[32,16,1024]{2,1,0:T(8,128)(2,1)}), bf16[32,16,1024]{2,1,0:T(8,128)(2,1)S(1)}, u32[]{:S(2)}, u32[]{:S(2)}) %all-to-all-start.2) | async-done | bytes 1048608 | tf_op jit(solution)/shard_map/all_to_all | solution.py:77
  117.6 0.5 convolution_bitcast_fusion
  118.1 0.0 copy-start.1
  118.1 1.2 fusion.2
  119.3 5.9 %all-to-all-start.3 = ((bf16[32,32,128]{2,1,0:T(8,128)(2,1)}), bf16[32,32,128]{2,1,0:T(8,128)(2,1)S(1)}, u32[]{:S(2)}, u32[]{:S(2)}) async-start(bf16[32,32,128]{2,1,0:T(8,128)(2,1)} %bitcast.12), calls=%async_computation.3 | async-start | bytes 524288 | tf_op jit(solution)/shard_map/all_to_all | solution.py:87
  125.3 0.5 fusion.40
  125.7 2.7 %fusion.4 = f32[128,4096]{1,0:T(8,128)S(1)} fusion(bf16[84,4096]{1,0:T(8,128)(2,1)} %param.20, bf16[128,4096]{1,0:T(8,128)(2,1)S(1)} %copy-done, bf16[4096,84]{0,1:T(8,128)(2,1)} %param.19, f32[128,84]{0,1:T(8,128)S(1)} %fusion.40), kind=kOutput, calls=%fused_computation.11 | convolution fusion | flops 176225280 | bytes 4564992 | tf_op jit(solution)/shard_map/dot_general | solution.py:12
  128.5 17.8 %all-to-all-done.3 = bf16[32,32,128]{2,1,0:T(8,128)(2,1)S(1)} async-done(((bf16[32,32,128]{2,1,0:T(8,128)(2,1)}), bf16[32,32,128]{2,1,0:T(8,128)(2,1)S(1)}, u32[]{:S(2)}, u32[]{:S(2)}) %all-to-all-start.3) | async-done | bytes 262176 | tf_op jit(solution)/shard_map/all_to_all | solution.py:87
  146.2 0.1 reduce_sum.47
  146.3 2.8 %convolution_add_fusion = f32[128,4096]{1,0:T(8,128)} fusion(f32[128,4096]{1,0:T(8,128)S(1)} %fusion.4, bf16[32,128]{1,0:T(8,128)(2,1)S(1)} %reduce_sum.47, bf16[32,4096]{1,0:T(8,128)(2,1)} %param.21), kind=kOutput, calls=%fused_computation | convolution fusion | flops 34078720 | bytes 4464640 | tf_op jit(solution)/shard_map/dot_general | solution.py:93
  149.0 1.9 reshape.88
  150.9 0.3 fusion.18
  151.2 1.9 %collective-permute-start = (bf16[16,4,4096]{2,1,0:T(4,128)(2,1)S(1)}, bf16[16,4,4096]{2,1,0:T(4,128)(2,1)S(1)}, u32[]{:S(2)}, u32[]{:S(2)}) collective-permute-start(bf16[16,4,4096]{2,1,0:T(4,128)(2,1)S(1)} %fusion.18), channel_id=1, source_target_pairs={{0,1},{1,0},{2,3},{3,2},{4,5},{5,4},{6,7},{7,6},{8,9},{9,8},{10,11... | collective-permute-start | bytes 1572872 | tf_op jit(solution)/shard_map/ppermute | solution.py:16
  153.1 1.9 collective-permute-done
  155.0 0.4 fusion.7
  155.4 34.4 %all_to_all.26 = bf16[16,4,4096]{2,1,0:T(4,128)(2,1)S(1)} all-to-all(bf16[16,4,4096]{2,1,0:T(4,128)(2,1)S(1)} %fusion.7), channel_id=1, replica_groups=mesh['expert'=32,'z'=16,'c'=2] {'z'}, dimensions={0} | all-to-all | bytes 1048576 | tf_op jit(solution)/shard_map/all_to_all | solution.py:101
  189.9 0.8 reduce_sum.48
  (8 shorter events, 0.0 us)
Async XLA Ops:
  0.0 1.2 copy-start
  0.0 22.1 %copy-start.3 = (s32[128,22]{0,1:T(8,128)S(1)}, s32[128,22]{0,1:T(8,128)}, u32[]{:S(2)}) copy-start(s32[128,22]{0,1:T(8,128)} %param.13) | copy-start | bytes 33796
  3.4 77.7 %copy-start.2 = (bf16[1,1024,336]{1,2,0:T(8,128)(2,1)S(1)}, bf16[1,1024,336]{1,2,0:T(8,128)(2,1)}, u32[]{:S(2)}) copy-start(bf16[1,1024,336]{1,2,0:T(8,128)(2,1)} %param.15) | copy-start | bytes 2064388
  3.4 39.7 %all-to-all-start = ((bf16[32,32,128]{2,1,0:T(8,128)(2,1)}), bf16[32,32,128]{2,1,0:T(8,128)(2,1)S(1)}, u32[]{:S(2)}, u32[]{:S(2)}) async-start(bf16[32,32,128]{2,1,0:T(8,128)(2,1)} %broadcast_in_dim.41), calls=%async_computation | async-start | bytes 524288 | tf_op jit(solution)/shard_map/all_to_all | solution.py:48
  85.2 5.7 %copy-start.4 = (f32[128,22]{0,1:T(8,128)S(1)}, f32[128,22]{0,1:T(8,128)}, u32[]{:S(2)}) copy-start(f32[128,22]{0,1:T(8,128)} %param.14) | copy-start | bytes 33796
  85.2 32.4 %all-to-all-start.2 = ((bf16[32,16,1024]{2,1,0:T(8,128)(2,1)}), bf16[32,16,1024]{2,1,0:T(8,128)(2,1)S(1)}, u32[]{:S(2)}, u32[]{:S(2)}) async-start(bf16[32,16,1024]{2,1,0:T(8,128)(2,1)} %bitcast.8), calls=%async_computation.2 | async-start | bytes 2097152 | tf_op jit(solution)/shard_map/all_to_all | solution.py:77
  118.1 7.2 %copy-start.1 = (bf16[4096,84]{0,1:T(8,128)(2,1)S(1)}, bf16[4096,84]{0,1:T(8,128)(2,1)}, u32[]{:S(2)}) copy-start(bf16[4096,84]{0,1:T(8,128)(2,1)} %param.18) | copy-start | bytes 2064388
  119.3 26.9 %all-to-all-start.3 = ((bf16[32,32,128]{2,1,0:T(8,128)(2,1)}), bf16[32,32,128]{2,1,0:T(8,128)(2,1)S(1)}, u32[]{:S(2)}, u32[]{:S(2)}) async-start(bf16[32,32,128]{2,1,0:T(8,128)(2,1)} %bitcast.12), calls=%async_computation.3 | async-start | bytes 524288 | tf_op jit(solution)/shard_map/all_to_all | solution.py:87
  151.2 3.8 %collective-permute-start = (bf16[16,4,4096]{2,1,0:T(4,128)(2,1)S(1)}, bf16[16,4,4096]{2,1,0:T(4,128)(2,1)S(1)}, u32[]{:S(2)}, u32[]{:S(2)}) collective-permute-start(bf16[16,4,4096]{2,1,0:T(4,128)(2,1)S(1)} %fusion.18), channel_id=1, source_target_pairs={{0,1},{1,0},{2,3},{3,2},{4,5},{5,4},{6,7},{7,6},{8,9},{9,8},{10,11... | collective-permute-start | bytes 1572872 | tf_op jit(solution)/shard_map/ppermute | solution.py:16

commit v2 on v1

v2 whole, which is shorter than its diff:
```python
import jax
import jax.numpy as jnp
from jax import lax
from jax.sharding import Mesh, PartitionSpec as P

CHIPS = ("i", "j", "k", "b")
TENSOR = CHIPS + ("c",)
BF16 = jnp.bfloat16
F32 = jnp.float32


def dot(a, b):
    return jnp.dot(a, b, preferred_element_type=F32)


def swap(value, axis):
    return lax.ppermute(value, axis, [(0, 1), (1, 0)])


def swap_cores(value):
    return swap(value, "c")


def fold(value, axis):
    me = lax.axis_index(axis)
    both = value.reshape((value.shape[0] // 2, 2) + value.shape[1:])
    given = swap(jnp.where(me == 0, both[:, 1], both[:, 0]).astype(BF16), axis)
    return jnp.where(me == 0, both[:, 0], both[:, 1]) + given.astype(F32)


def shards(
    hidden_in,
    w_latent,
    routes,
    gates,
    expert_gate,
    expert_up,
    expert_down,
    shared_gate,
    shared_up,
    shared_down,
    w_restore,
):
    groups = lax.axis_size("expert")
    chips = lax.axis_size(CHIPS)
    cores = lax.axis_size("c")
    tensor_size = chips * cores
    core = lax.axis_index("c")
    position = lax.axis_index(TENSOR)
    rows = hidden_in.shape[0]
    block = w_restore.shape[0]
    width = block * tensor_size
    model = hidden_in.shape[1]
    top = routes.shape[1]
    experts = groups * tensor_size // 4
    capacity = 4 * max(1, 3 * rows * top // (8 * experts))

    half = block * chips

    own = rows // tensor_size
    wide = model // cores
    restore = lax.all_gather(
        jnp.pad(w_restore, ((0, 0), (0, 1024))), CHIPS, axis=0, tiled=True
    )

    latent_cols = dot(hidden_in, w_latent).astype(BF16)
    copies = jnp.broadcast_to(latent_cols.T[None], (chips, block, rows))
    latent_t = lax.all_to_all(copies, CHIPS, 0, 0, tiled=True).reshape(half, rows)

    place = lax.broadcasted_iota(jnp.int32, (half, width), 0)
    column = lax.broadcasted_iota(jnp.int32, (half, width), 1)
    first = (place // block) * (cores * block) + place % block

    def choose(which):
        return (column == first + which * block).astype(BF16)

    mine, theirs = choose(core), choose(1 - core)

    targets = jnp.arange(groups, dtype=jnp.int32) * (tensor_size // 4) + position // 4
    matched = routes[:, :, None] == targets[None, None, :]
    hits = jnp.sum(matched.astype(BF16), axis=1)
    below = (
        lax.broadcasted_iota(jnp.int32, (rows, rows), 0)
        > lax.broadcasted_iota(jnp.int32, (rows, rows), 1)
    ).astype(BF16)
    earlier = dot(below, hits)
    slots = jnp.where(hits > 0.5, earlier, -1.0).T
    slot_ids = jnp.arange(capacity, dtype=F32)
    slot_mask = slots[:, None, :] == slot_ids[None, :, None]
    pick = slot_mask.astype(BF16).reshape(groups * capacity, rows)

    gate = [dot(m, expert_gate[0]).astype(BF16) for m in (mine, theirs)]
    latent_t, gate = lax.optimization_barrier((latent_t, gate))
    gate_mine, gate_theirs = gate
    outbound = lax.dot_general(
        pick, latent_t, (((1,), (1,)), ((), ())), preferred_element_type=F32
    ).astype(BF16)
    outbound, expert_up, expert_down = lax.optimization_barrier(
        (outbound, expert_up, expert_down)
    )
    taken = lax.all_to_all(
        outbound.reshape(groups, capacity, half), "expert", 0, 0, tiled=True
    ).reshape(groups * capacity, half)

    up = [dot(m, expert_up[0]).astype(BF16) for m in (mine, theirs)]
    down = [dot(expert_down[0], m.T).astype(BF16) for m in (mine, theirs)]
    shared_act = (
        jax.nn.silu(dot(hidden_in, shared_gate)) * dot(hidden_in, shared_up)
    ).astype(BF16)
    total = dot(shared_act, shared_down)
    left, right = total[:, :wide], total[:, wide:]
    given = swap_cores(jnp.where(core == 0, right, left).astype(BF16))
    pair = jnp.where(core == 0, left, right) + given.astype(F32)
    folded = fold(pair.reshape(chips, cores * own, wide), "b")
    taken, up, down = lax.optimization_barrier((taken, up, down))
    up_mine, up_theirs = up
    down_mine, down_theirs = down
    other = swap_cores(taken)
    gate_act = dot(taken, gate_mine) + dot(other, gate_theirs)
    up_act = dot(taken, up_mine) + dot(other, up_theirs)
    act = (jax.nn.silu(gate_act) * up_act).astype(BF16)
    received = swap_cores(dot(act, down_theirs).astype(BF16))
    part = (dot(act, down_mine) + received.astype(F32)).astype(BF16)
    part, routes_later, folded = lax.optimization_barrier((part, routes, folded))
    returned = lax.all_to_all(
        part.reshape(groups, capacity, half), "expert", 0, 0, tiled=True
    ).reshape(groups * capacity, half)

    folded = fold(folded, "k")
    folded = fold(folded, "j")
    matched = routes_later[:, :, None] == targets[None, None, :]
    weight = jnp.sum(jnp.where(matched, gates[:, :, None], 0.0), axis=1)
    weighted = jnp.where(slot_mask, weight.T[:, None, :], 0.0).reshape(groups * capacity, rows)
    weighted_high = weighted.astype(BF16)
    weighted_low = (weighted - weighted_high.astype(F32)).astype(BF16)
    returned, restore, folded, weighted_high, weighted_low = lax.optimization_barrier(
        (returned, restore, folded, weighted_high, weighted_low)
    )

    def combine(w):
        return lax.dot_general(
            w, returned, (((0,), (0,)), ((), ())), preferred_element_type=F32
        )

    routed_terms = (combine(weighted_high) + combine(weighted_low)).astype(BF16)
    pieces = lax.all_to_all(
        routed_terms.reshape(chips, cores * own, half), CHIPS, 0, 0, tiled=True
    )
    routed = jnp.sum(pieces.astype(F32), axis=0).astype(BF16)
    shared_sum = fold(folded, "i")[0]
    restored = dot(routed, restore)[:, :model]
    blank = jnp.zeros_like(shared_sum)
    both = restored + jnp.concatenate(
        [jnp.where(core == 0, shared_sum, blank), jnp.where(core == 0, blank, shared_sum)], axis=1
    )
    kept = jnp.where(core == 0, both[:own], both[own:])
    given = swap_cores(jnp.where(core == 0, both[own:], both[:own]).astype(BF16))
    return (kept + given.astype(F32)).astype(BF16)


def solution(mesh):
    shape = mesh.devices.shape
    split = Mesh(
        mesh.devices.reshape((shape[0],) + (2,) * len(TENSOR)), ("expert",) + TENSOR
    )
    both = ("expert",) + TENSOR
    in_specs = (
        P("expert", None),
        P(None, TENSOR),
        P("expert", None),
        P("expert", None),
        P(both, None, None),
        P(both, None, None),
        P(both, None, None),
        P(None, TENSOR),
        P(None, TENSOR),
        P(TENSOR, None),
        P(TENSOR, None),
    )
    return jax.shard_map(
        shards, mesh=split, in_specs=in_specs, out_specs=P(both, None), check_vma=False
    )
```

time: 191 us -> 159 us (0.83)
  the two profiles are of different devices: /device:TPU:66 before, /device:TPU:1 now
where the time goes in v2:
time: 159 us; the launch traced here: 158 us
  starting transfers between devices  88.9 us (56%)
  matrix products  30.6 us (19%)
  waiting for transfers between devices  16 us (10%)
  between operations  13.9 us (9%)
  other arithmetic  4.65 us (3%)
  local copies, waits for them, and re-layouts  4.33 us (3%)
    ppermute x8, starting transfers between devices, swap(): return lax.ppermute(value, axis, [(0, 1), (1, 0)])  42 us
    dot_general x17, matrix products, dot(): return jnp.dot(a, b, preferred_element_type=F32)  28.3 us
    all_to_all x1, starting transfers between devices, shards(): lax.all_to_all(copies, CHIPS, 0, 0, tiled=True).reshape(half, rows)  19.4 us
    ppermute x8, waiting for transfers between devices, swap(): return lax.ppermute(value, axis, [(0, 1), (1, 0)])  15.9 us
    all_to_all x1, starting transfers between devices, shards(): lax.all_to_all(routed_terms.reshape(chips, cores * own, half), CHIPS, 0,...  11.3 us
    all_to_all x1, starting transfers between devices, shards(): lax.all_to_all(outbound.reshape(groups, capacity, half), 'expert', 0, 0,...  9.79 us
    all_to_all x1, starting transfers between devices, shards(): lax.all_to_all(part.reshape(groups, capacity, half), 'expert', 0, 0, tile...  6.33 us
  transfers between devices with their start and end apart: 13, of which 5 were waited for; matrix products, arithmetic and copies ran while one was open for 20% of the time, Pallas kernels for 0%

profile of v2, /device:TPU:1, one launch (start us, length us, event | category | flops | bytes accessed | tf_op | source)
XLA Modules:
  0.0 158.3 jit_solution(6912785240902208321)
XLA Ops:
  6.5 1.8 %pad.4 = bf16[32,5120]{1,0:T(8,128)(2,1)} pad(bf16[32,4096]{1,0:T(8,128)(2,1)} %param.21, bf16[]{:T(256)} %constant.82.clone.1), padding=0_0x0_1024 | pad | bytes 589826 | tf_op jit(solution)/shard_map/jit(_pad)/pad | solution.py:63
  8.4 1.4 convolution_convert_fusion.8
  10.5 19.4 %all-to-all-start = ((bf16[16,32,128]{2,1,0:T(8,128)(2,1)}), bf16[16,32,128]{2,1,0:T(8,128)(2,1)S(1)}, u32[]{:S(2)}, u32[]{:S(2)}) async-start(bf16[16,32,128]{2,1,0:T(8,128)(2,1)} %broadcast_in_dim.48), calls=%async_computation | async-start | bytes 262144 | tf_op jit(solution)/shard_map/all_to_all | solution.py:68
  30.4 2.7 %fusion.4 = f32[128,4096]{1,0:T(8,128)S(1)} fusion(bf16[84,4096]{1,0:T(8,128)(2,1)} %param.20, bf16[128,4096]{1,0:T(8,128)(2,1)S(1)} %copy-done, bf16[4096,84]{0,1:T(8,128)(2,1)} %param.19, f32[128,84]{0,1:T(8,128)S(1)} %fusion.36), kind=kOutput, calls=%fused_computation.20 | convolution fusion | flops 176225280 | bytes 4564992 | tf_op jit(solution)/shard_map/dot_general | solution.py:13
  34.0 2.9 %collective-permute-start.2 = (bf16[128,2048]{1,0:T(8,128)(2,1)}, bf16[128,2048]{1,0:T(8,128)(2,1)}, u32[]{:S(2)}, u32[]{:S(2)}) collective-permute-start(bf16[128,2048]{1,0:T(8,128)(2,1)} %select_convert_fusion), channel_id=1, source_target_pairs={{0,1},{1,0},{2,3},{3,2},{4,5},{5,4},{6,7},{7,6},{8,9},{9,8},{10,11... | collective-permute-start | bytes 1572872 | tf_op jit(solution)/shard_map/ppermute | solution.py:17
  37.5 3.2 %convolution_convert_fusion.6 = bf16[512,336]{0,1:T(8,128)(2,1)} fusion(bf16[1,1024,336]{1,2,0:T(8,128)(2,1)} %param.15, s32[]{:T(128)S(6)} %mul.59, s32[512]{0:T(512)S(1)} %get-tuple-element.46, s32[512]{0:T(512)S(1)} %get-tuple-element.47, s32[512]{0:T(512)S(1)} %get-tuple-element.45, s32[512]{0:T(512)S(1)} %get-tuple-element.48, ...), kind=kOutput, calls=%fused_computation.13 | convolution fusion | flops 355639296 | bytes 1041412 | tf_op jit(solution)/shard_map/dot_general | solution.py:13
  40.7 1.9 %convolution_convert_fusion.7 = bf16[512,336]{0,1:T(8,128)(2,1)} fusion(bf16[1,1024,336]{1,2,0:T(8,128)(2,1)S(1)} %copy-done.8, s32[]{:T(128)S(6)} %mul.58, s32[512]{0:T(512)S(1)} %get-tuple-element.46, s32[512]{0:T(512)S(1)} %get-tuple-element.47, s32[512]{0:T(512)S(1)} %get-tuple-element.45, s32[512]{0:T(512)S(1)} %get-tuple-element.48, ...), kind=kOutput, calls=%fused_computation.14 | convolution fusion | flops 355639296 | bytes 1041412 | tf_op jit(solution)/shard_map/dot_general | solution.py:13
  42.6 1.1 convolution_convert_fusion.1
  43.7 9.8 %all-to-all-start.1 = ((bf16[32,16,512]{2,1,0:T(8,128)(2,1)}), bf16[32,16,512]{2,1,0:T(8,128)(2,1)}, u32[]{:S(2)}, u32[]{:S(2)}) async-start(bf16[32,16,512]{2,1,0:T(8,128)(2,1)} %bitcast.152), calls=%async_computation.1 | async-start | bytes 1048576 | tf_op jit(solution)/shard_map/all_to_all | solution.py:101
  53.5 3.1 %convolution_convert_fusion.2 = bf16[336,512]{1,0:T(8,128)(2,1)} fusion(bf16[1,336,1024]{2,1,0:T(8,128)(2,1)} %param.17, s32[]{:T(128)S(6)} %mul.59, s32[512]{0:T(512)S(1)} %get-tuple-element.46, s32[512]{0:T(512)S(1)} %get-tuple-element.47, s32[512]{0:T(512)S(1)} %get-tuple-element.45, s32[512]{0:T(512)S(1)} %get-tuple-element.48, ...), kind=kOutput, calls=%fused_computation.9 | convolution fusion | flops 355639296 | bytes 1041412 | tf_op jit(solution)/shard_map/dot_general | solution.py:13
  56.6 1.3 convolution_convert_fusion.3
  57.9 1.9 %convolution_convert_fusion.4 = bf16[512,336]{0,1:T(8,128)(2,1)} fusion(bf16[1,1024,336]{1,2,0:T(8,128)(2,1)S(1)} %copy-done.10, s32[]{:T(128)S(6)} %mul.59, s32[512]{0:T(512)S(1)} %get-tuple-element.46, s32[512]{0:T(512)S(1)} %get-tuple-element.47, s32[512]{0:T(512)S(1)} %get-tuple-element.45, s32[512]{0:T(512)S(1)} %get-tuple-element.48, ...), kind=kOutput, calls=%fused_computation.11 | convolution fusion | flops 355639296 | bytes 1041412 | tf_op jit(solution)/shard_map/dot_general | solution.py:13
  59.9 1.9 %convolution_convert_fusion.5 = bf16[512,336]{0,1:T(8,128)(2,1)} fusion(bf16[1,1024,336]{1,2,0:T(8,128)(2,1)S(1)} %copy-done.10, s32[]{:T(128)S(6)} %mul.58, s32[512]{0:T(512)S(1)} %get-tuple-element.46, s32[512]{0:T(512)S(1)} %get-tuple-element.47, s32[512]{0:T(512)S(1)} %get-tuple-element.45, s32[512]{0:T(512)S(1)} %get-tuple-element.48, ...), kind=kOutput, calls=%fused_computation.12 | convolution fusion | flops 355639296 | bytes 1041412 | tf_op jit(solution)/shard_map/dot_general | solution.py:13
  61.8 1.2 convert_add_fusion
  64.0 3.5 %collective-permute-start.3 = (bf16[8,8,2048]{2,1,0:T(8,128)(2,1)S(1)}, bf16[8,8,2048]{2,1,0:T(8,128)(2,1)}, u32[]{:S(2)}, u32[]{:S(2)}) collective-permute-start(bf16[8,8,2048]{2,1,0:T(8,128)(2,1)S(1)} %fusion.11), channel_id=1, source_target_pairs={{0,2},{2,0},{1,3},{3,1},{4,6},{6,4},{5,7},{7,5},{8,10},{10,8},{9,1... | collective-permute-start | bytes 786440 | tf_op jit(solution)/shard_map/ppermute | solution.py:17
  67.5 6.8 %collective-permute-start = (bf16[512,512]{1,0:T(8,128)(2,1)}, bf16[512,512]{1,0:T(8,128)(2,1)S(1)}, u32[]{:S(2)}, u32[]{:S(2)}) collective-permute-start(bf16[512,512]{1,0:T(8,128)(2,1)} %bitcast.5), channel_id=1, source_target_pairs={{0,1},{1,0},{2,3},{3,2},{4,5},{5,4},{6,7},{7,6},{8,9},{9,8},{10,11... | collective-permute-start | bytes 1572872 | tf_op jit(solution)/shard_map/ppermute | solution.py:17
  74.3 1.5 fusion.35
  75.9 1.5 fusion.34
  79.0 1.3 convolution_convert_fusion
  80.3 1.9 %collective-permute-start.1 = (bf16[512,512]{1,0:T(8,128)(2,1)}, bf16[512,512]{1,0:T(8,128)(2,1)S(1)}, u32[]{:S(2)}, u32[]{:S(2)}) collective-permute-start(bf16[512,512]{1,0:T(8,128)(2,1)} %convolution_convert_fusion), channel_id=1, source_target_pairs={{0,1},{1,0},{2,3},{3,2},{4,5},{5,4},{6,7},{7,6},{8,9},{9,8},{10,11... | collective-permute-start | bytes 1572872 | tf_op jit(solution)/shard_map/ppermute | solution.py:17
  82.2 1.0 bitcast_add_fusion
  84.3 2.2 %add_convert_fusion = bf16[512,512]{1,0:T(8,128)(2,1)} fusion(bf16[512,512]{1,0:T(8,128)(2,1)S(1)} %collective-permute-done.1, bf16[512,336]{0,1:T(8,128)(2,1)} %copy-done.5, bf16[336,512]{1,0:T(8,128)(2,1)S(1)} %convolution_convert_fusion.3), kind=kOutput, calls=%fused_computation.25 | convolution fusion | flops 176947200 | bytes 1736704 | tf_op jit(solution)/shard_map/dot_general | solution.py:13
  86.6 4.2 %collective-permute-start.4 = (bf16[4,8,2048]{2,1,0:T(8,128)(2,1)S(1)}, bf16[4,8,2048]{2,1,0:T(8,128)(2,1)S(1)}, u32[]{:S(2)}, u32[]{:S(2)}) collective-permute-start(bf16[4,8,2048]{2,1,0:T(8,128)(2,1)S(1)} %fusion.18), channel_id=1, source_target_pairs={{0,4},{4,0},{1,5},{5,1},{2,6},{6,2},{3,7},{7,3},{8,12},{12,8},{9,1... | collective-permute-start | bytes 393224 | tf_op jit(solution)/shard_map/ppermute | solution.py:17
  90.8 6.3 %all-to-all-start.2 = ((bf16[32,16,512]{2,1,0:T(8,128)(2,1)}), bf16[32,16,512]{2,1,0:T(8,128)(2,1)S(1)}, u32[]{:S(2)}, u32[]{:S(2)}) async-start(bf16[32,16,512]{2,1,0:T(8,128)(2,1)} %bitcast.11), calls=%async_computation.2 | async-start | bytes 1048576 | tf_op jit(solution)/shard_map/all_to_all | solution.py:125
  97.2 2.9 %collective-permute-done.4 = bf16[4,8,2048]{2,1,0:T(8,128)(2,1)S(1)} collective-permute-done((bf16[4,8,2048]{2,1,0:T(8,128)(2,1)S(1)}, bf16[4,8,2048]{2,1,0:T(8,128)(2,1)S(1)}, u32[]{:S(2)}, u32[]{:S(2)}) %collective-permute-start.4) | collective-permute-done | bytes 131104 | tf_op jit(solution)/shard_map/ppermute | solution.py:17
  100.1 7.0 %collective-permute-start.5 = (bf16[2,8,2048]{2,1,0:T(8,128)(2,1)S(1)}, bf16[2,8,2048]{2,1,0:T(8,128)(2,1)S(1)}, u32[]{:S(2)}, u32[]{:S(2)}) collective-permute-start(bf16[2,8,2048]{2,1,0:T(8,128)(2,1)S(1)} %fusion.19), channel_id=1, source_target_pairs={{0,8},{8,0},{1,9},{9,1},{2,10},{10,2},{3,11},{11,3},{4,12},{12,4},... | collective-permute-start | bytes 196616 | tf_op jit(solution)/shard_map/ppermute | solution.py:17
  107.6 5.7 %collective-permute-done.5 = bf16[2,8,2048]{2,1,0:T(8,128)(2,1)S(1)} collective-permute-done((bf16[2,8,2048]{2,1,0:T(8,128)(2,1)S(1)}, bf16[2,8,2048]{2,1,0:T(8,128)(2,1)S(1)}, u32[]{:S(2)}, u32[]{:S(2)}) %collective-permute-start.5) | collective-permute-done | bytes 65568 | tf_op jit(solution)/shard_map/ppermute | solution.py:17
  114.5 11.3 %all-to-all-start.3 = ((bf16[16,8,512]{2,1,0:T(8,128)(2,1)}), bf16[16,8,512]{2,1,0:T(8,128)(2,1)S(1)}, u32[]{:S(2)}, u32[]{:S(2)}) async-start(bf16[16,8,512]{2,1,0:T(8,128)(2,1)} %fusion.2), calls=%async_computation.3 | async-start | bytes 262144 | tf_op jit(solution)/shard_map/all_to_all | solution.py:146
  125.8 12.0 %collective-permute-start.6 = (bf16[1,8,2048]{2,1,0:T(8,128)(2,1)S(1)}, bf16[1,8,2048]{2,1,0:T(8,128)(2,1)S(1)}, u32[]{:S(2)}, u32[]{:S(2)}) collective-permute-start(bf16[1,8,2048]{2,1,0:T(8,128)(2,1)S(1)} %fusion.25), channel_id=1, source_target_pairs={{0,16},{16,0},{1,17},{17,1},{2,18},{18,2},{3,19},{19,3},{4,20},{20... | collective-permute-start | bytes 98312 | tf_op jit(solution)/shard_map/ppermute | solution.py:17
  137.8 5.5 %collective-permute-done.6 = bf16[1,8,2048]{2,1,0:T(8,128)(2,1)S(1)} collective-permute-done((bf16[1,8,2048]{2,1,0:T(8,128)(2,1)S(1)}, bf16[1,8,2048]{2,1,0:T(8,128)(2,1)S(1)}, u32[]{:S(2)}, u32[]{:S(2)}) %collective-permute-start.6) | collective-permute-done | bytes 32800 | tf_op jit(solution)/shard_map/ppermute | solution.py:17
  143.4 2.8 %convolution_add_fusion = f32[8,4096]{1,0:T(8,128)S(1)} fusion(bf16[8,512]{1,0:T(8,128)(2,1)S(1)} %reduce_sum.35, bf16[512,5120]{1,0:T(8,128)(2,1)} %all-gather.2.cloned.1.call-done, f32[8,2048]{1,0:T(8,128)S(1)} %get-tuple-element.44, f32[8,2048]{1,0:T(8,128)S(1)} %get-tuple-element.43), kind=kOutput, calls=%fused_computation | convolution fusion | flops 33619968 | bytes 4464640 | tf_op jit(solution)/shard_map/dot_general | solution.py:13
  146.3 3.7 %collective-permute-start.7 = (bf16[4,4096]{1,0:T(4,128)(2,1)S(1)}, bf16[4,4096]{1,0:T(4,128)(2,1)S(1)}, u32[]{:S(2)}, u32[]{:S(2)}) collective-permute-start(bf16[4,4096]{1,0:T(4,128)(2,1)S(1)} %select_convert_fusion.4), channel_id=1, source_target_pairs={{0,1},{1,0},{2,3},{3,2},{4,5},{5,4},{6,7},{7,6},{8,9},{9,8},{10,11... | collective-permute-start | bytes 98312 | tf_op jit(solution)/shard_map/ppermute | solution.py:17
  (67 shorter events, 9.4 us)
Async XLA Ops:
  6.5 1.8 %copy-start = (bf16[128,4096]{1,0:T(8,128)(2,1)S(1)}, bf16[128,4096]{1,0:T(8,128)(2,1)}, u32[]{:S(2)}) copy-start(bf16[128,4096]{1,0:T(8,128)(2,1)} %param.11) | copy-start | bytes 3145732
  6.5 23.4 %copy-start.3 = (bf16[4096,84]{0,1:T(8,128)(2,1)S(1)}, bf16[4096,84]{0,1:T(8,128)(2,1)}, u32[]{:S(2)}) copy-start(bf16[4096,84]{0,1:T(8,128)(2,1)} %param.18) | copy-start | bytes 2064388
  6.5 106.7 %all-gather.2.cloned.1.call-start = ((), (), s32[]{:S(2)}) async-start(), calls=%async_computation.4 | async-start | bytes 5570560 | tf_op jit(solution)/shard_map/all_gather | solution.py:62
  10.5 32.1 %all-to-all-start = ((bf16[16,32,128]{2,1,0:T(8,128)(2,1)}), bf16[16,32,128]{2,1,0:T(8,128)(2,1)S(1)}, u32[]{:S(2)}, u32[]{:S(2)}) async-start(bf16[16,32,128]{2,1,0:T(8,128)(2,1)} %broadcast_in_dim.48), calls=%async_computation | async-start | bytes 262144 | tf_op jit(solution)/shard_map/all_to_all | solution.py:68
  30.4 6.6 %copy-start.6 = (s32[128,22]{0,1:T(8,128)S(1)}, s32[128,22]{0,1:T(8,128)}, u32[]{:S(2)}) copy-start(s32[128,22]{0,1:T(8,128)} %param.13) | copy-start | bytes 33796
  34.0 27.7 %collective-permute-start.2 = (bf16[128,2048]{1,0:T(8,128)(2,1)}, bf16[128,2048]{1,0:T(8,128)(2,1)}, u32[]{:S(2)}, u32[]{:S(2)}) collective-permute-start(bf16[128,2048]{1,0:T(8,128)(2,1)} %select_convert_fusion), channel_id=1, source_target_pairs={{0,1},{1,0},{2,3},{3,2},{4,5},{5,4},{6,7},{7,6},{8,9},{9,8},{10,11... | collective-permute-start | bytes 1572872 | tf_op jit(solution)/shard_map/ppermute | solution.py:17
  37.5 3.2 %copy-start.8 = (bf16[1,1024,336]{1,2,0:T(8,128)(2,1)S(1)}, bf16[1,1024,336]{1,2,0:T(8,128)(2,1)}, u32[]{:S(2)}) copy-start(bf16[1,1024,336]{1,2,0:T(8,128)(2,1)} %param.15) | copy-start | bytes 2064388
  43.7 23.9 %all-to-all-start.1 = ((bf16[32,16,512]{2,1,0:T(8,128)(2,1)}), bf16[32,16,512]{2,1,0:T(8,128)(2,1)}, u32[]{:S(2)}, u32[]{:S(2)}) async-start(bf16[32,16,512]{2,1,0:T(8,128)(2,1)} %bitcast.152), calls=%async_computation.1 | async-start | bytes 1048576 | tf_op jit(solution)/shard_map/all_to_all | solution.py:101
  53.5 3.2 %copy-start.9 = (bf16[1,336,1024]{2,1,0:T(8,128)(2,1)S(1)}, bf16[1,336,1024]{2,1,0:T(8,128)(2,1)}, u32[]{:S(2)}) copy-start(bf16[1,336,1024]{2,1,0:T(8,128)(2,1)} %param.17) | copy-start | bytes 2064388
  56.6 1.3 copy-start.10
  63.0 1.0 copy-start.1
  63.0 14.4 %copy-start.4 = (bf16[512,336]{0,1:T(8,128)(2,1)S(1)}, bf16[512,336]{0,1:T(8,128)(2,1)}, u32[]{:S(2)}) copy-start(bf16[512,336]{0,1:T(8,128)(2,1)} %convolution_convert_fusion.6) | copy-start | bytes 1032196
  64.0 18.2 %collective-permute-start.3 = (bf16[8,8,2048]{2,1,0:T(8,128)(2,1)S(1)}, bf16[8,8,2048]{2,1,0:T(8,128)(2,1)}, u32[]{:S(2)}, u32[]{:S(2)}) collective-permute-start(bf16[8,8,2048]{2,1,0:T(8,128)(2,1)S(1)} %fusion.11), channel_id=1, source_target_pairs={{0,2},{2,0},{1,3},{3,1},{4,6},{6,4},{5,7},{7,5},{8,10},{10,8},{9,1... | collective-permute-start | bytes 786440 | tf_op jit(solution)/shard_map/ppermute | solution.py:17
  67.5 9.9 %collective-permute-start = (bf16[512,512]{1,0:T(8,128)(2,1)}, bf16[512,512]{1,0:T(8,128)(2,1)S(1)}, u32[]{:S(2)}, u32[]{:S(2)}) collective-permute-start(bf16[512,512]{1,0:T(8,128)(2,1)} %bitcast.5), channel_id=1, source_target_pairs={{0,1},{1,0},{2,3},{3,2},{4,5},{5,4},{6,7},{7,6},{8,9},{9,8},{10,11... | collective-permute-start | bytes 1572872 | tf_op jit(solution)/shard_map/ppermute | solution.py:17
  75.9 2.0 %copy-start.12 = (bf16[512,336]{0,1:T(8,128)(2,1)S(1)}, bf16[512,336]{0,1:T(8,128)(2,1)}, u32[]{:S(2)}) copy-start(bf16[512,336]{0,1:T(8,128)(2,1)} %convolution_convert_fusion.4) | copy-start | bytes 1032196
  77.8 1.2 copy-start.11
  77.8 4.4 %copy-start.2 = (f32[128,2048]{1,0:T(8,128)S(1)}, f32[128,2048]{1,0:T(8,128)}, u32[]{:S(2)}) copy-start(f32[128,2048]{1,0:T(8,128)} %copy-done.1) | copy-start | bytes 3145732
  78.3 0.7 copy-start.5
  80.3 4.0 %collective-permute-start.1 = (bf16[512,512]{1,0:T(8,128)(2,1)}, bf16[512,512]{1,0:T(8,128)(2,1)S(1)}, u32[]{:S(2)}, u32[]{:S(2)}) collective-permute-start(bf16[512,512]{1,0:T(8,128)(2,1)} %convolution_convert_fusion), channel_id=1, source_target_pairs={{0,1},{1,0},{2,3},{3,2},{4,5},{5,4},{6,7},{7,6},{8,9},{9,8},{10,11... | collective-permute-start | bytes 1572872 | tf_op jit(solution)/shard_map/ppermute | solution.py:17
  83.3 23.9 %copy-start.7 = (f32[128,22]{0,1:T(8,128)S(1)}, f32[128,22]{0,1:T(8,128)}, u32[]{:S(2)}) copy-start(f32[128,22]{0,1:T(8,128)} %param.14) | copy-start | bytes 33796
  86.6 13.5 %collective-permute-start.4 = (bf16[4,8,2048]{2,1,0:T(8,128)(2,1)S(1)}, bf16[4,8,2048]{2,1,0:T(8,128)(2,1)S(1)}, u32[]{:S(2)}, u32[]{:S(2)}) collective-permute-start(bf16[4,8,2048]{2,1,0:T(8,128)(2,1)S(1)} %fusion.18), channel_id=1, source_target_pairs={{0,4},{4,0},{1,5},{5,1},{2,6},{6,2},{3,7},{7,3},{8,12},{12,8},{9,1... | collective-permute-start | bytes 393224 | tf_op jit(solution)/shard_map/ppermute | solution.py:17
  90.8 22.4 %all-to-all-start.2 = ((bf16[32,16,512]{2,1,0:T(8,128)(2,1)}), bf16[32,16,512]{2,1,0:T(8,128)(2,1)S(1)}, u32[]{:S(2)}, u32[]{:S(2)}) async-start(bf16[32,16,512]{2,1,0:T(8,128)(2,1)} %bitcast.11), calls=%async_computation.2 | async-start | bytes 1048576 | tf_op jit(solution)/shard_map/all_to_all | solution.py:125
  100.1 13.1 %collective-permute-start.5 = (bf16[2,8,2048]{2,1,0:T(8,128)(2,1)S(1)}, bf16[2,8,2048]{2,1,0:T(8,128)(2,1)S(1)}, u32[]{:S(2)}, u32[]{:S(2)}) collective-permute-start(bf16[2,8,2048]{2,1,0:T(8,128)(2,1)S(1)} %fusion.19), channel_id=1, source_target_pairs={{0,8},{8,0},{1,9},{9,1},{2,10},{10,2},{3,11},{11,3},{4,12},{12,4},... | collective-permute-start | bytes 196616 | tf_op jit(solution)/shard_map/ppermute | solution.py:17
  114.5 28.9 %all-to-all-start.3 = ((bf16[16,8,512]{2,1,0:T(8,128)(2,1)}), bf16[16,8,512]{2,1,0:T(8,128)(2,1)S(1)}, u32[]{:S(2)}, u32[]{:S(2)}) async-start(bf16[16,8,512]{2,1,0:T(8,128)(2,1)} %fusion.2), calls=%async_computation.3 | async-start | bytes 262144 | tf_op jit(solution)/shard_map/all_to_all | solution.py:146
  125.8 17.5 %collective-permute-start.6 = (bf16[1,8,2048]{2,1,0:T(8,128)(2,1)S(1)}, bf16[1,8,2048]{2,1,0:T(8,128)(2,1)S(1)}, u32[]{:S(2)}, u32[]{:S(2)}) collective-permute-start(bf16[1,8,2048]{2,1,0:T(8,128)(2,1)S(1)} %fusion.25), channel_id=1, source_target_pairs={{0,16},{16,0},{1,17},{17,1},{2,18},{18,2},{3,19},{19,3},{4,20},{20... | collective-permute-start | bytes 98312 | tf_op jit(solution)/shard_map/ppermute | solution.py:17
  146.3 4.5 %collective-permute-start.7 = (bf16[4,4096]{1,0:T(4,128)(2,1)S(1)}, bf16[4,4096]{1,0:T(4,128)(2,1)S(1)}, u32[]{:S(2)}, u32[]{:S(2)}) collective-permute-start(bf16[4,4096]{1,0:T(4,128)(2,1)S(1)} %select_convert_fusion.4), channel_id=1, source_target_pairs={{0,1},{1,0},{2,3},{3,2},{4,5},{5,4},{6,7},{7,6},{8,9},{9,8},{10,11... | collective-permute-start | bytes 98312 | tf_op jit(solution)/shard_map/ppermute | solution.py:17
Sparse Core Ops, SparseCore 0:
  10.0 98.7 all-gather.1

commit v3 on v2

--- a/solution.py
+++ b/solution.py
@@ -19,13 +19,6 @@
 
 def swap_cores(value):
     return swap(value, "c")
-
-
-def fold(value, axis):
-    me = lax.axis_index(axis)
-    both = value.reshape((value.shape[0] // 2, 2) + value.shape[1:])
-    given = swap(jnp.where(me == 0, both[:, 1], both[:, 0]).astype(BF16), axis)
-    return jnp.where(me == 0, both[:, 0], both[:, 1]) + given.astype(F32)
 
 
 def shards(
@@ -60,7 +53,7 @@
     own = rows // tensor_size
     wide = model // cores
     restore = lax.all_gather(
-        jnp.pad(w_restore, ((0, 0), (0, 1024))), CHIPS, axis=0, tiled=True
+        jnp.pad(w_restore, ((0, 0), (0, 512))), CHIPS, axis=0, tiled=True
     )
 
     latent_cols = dot(hidden_in, w_latent).astype(BF16)
@@ -111,8 +104,9 @@
     left, right = total[:, :wide], total[:, wide:]
     given = swap_cores(jnp.where(core == 0, right, left).astype(BF16))
     pair = jnp.where(core == 0, left, right) + given.astype(F32)
-    folded = fold(pair.reshape(chips, cores * own, wide), "b")
-    taken, up, down = lax.optimization_barrier((taken, up, down))
+    pair = pair.astype(BF16)
+    taken, up, down, pair = lax.optimization_barrier((taken, up, down, pair))
+    shared_sum = lax.psum_scatter(pair, CHIPS, scatter_dimension=0, tiled=True)
     up_mine, up_theirs = up
     down_mine, down_theirs = down
     other = swap_cores(taken)
@@ -121,20 +115,18 @@
     act = (jax.nn.silu(gate_act) * up_act).astype(BF16)
     received = swap_cores(dot(act, down_theirs).astype(BF16))
     part = (dot(act, down_mine) + received.astype(F32)).astype(BF16)
-    part, routes_later, folded = lax.optimization_barrier((part, routes, folded))
+    part, routes_later = lax.optimization_barrier((part, routes))
     returned = lax.all_to_all(
         part.reshape(groups, capacity, half), "expert", 0, 0, tiled=True
     ).reshape(groups * capacity, half)
 
-    folded = fold(folded, "k")
-    folded = fold(folded, "j")
     matched = routes_later[:, :, None] == targets[None, None, :]
     weight = jnp.sum(jnp.where(matched, gates[:, :, None], 0.0), axis=1)
     weighted = jnp.where(slot_mask, weight.T[:, None, :], 0.0).reshape(groups * capacity, rows)
     weighted_high = weighted.astype(BF16)
     weighted_low = (weighted - weighted_high.astype(F32)).astype(BF16)
-    returned, restore, folded, weighted_high, weighted_low = lax.optimization_barrier(
-        (returned, restore, folded, weighted_high, weighted_low)
+    returned, restore, weighted_high, weighted_low = lax.optimization_barrier(
+        (returned, restore, weighted_high, weighted_low)
     )
 
     def combine(w):
@@ -147,7 +139,7 @@
         routed_terms.reshape(chips, cores * own, half), CHIPS, 0, 0, tiled=True
     )
     routed = jnp.sum(pieces.astype(F32), axis=0).astype(BF16)
-    shared_sum = fold(folded, "i")[0]
+    shared_sum = shared_sum.astype(F32)
     restored = dot(routed, restore)[:, :model]
     blank = jnp.zeros_like(shared_sum)
     both = restored + jnp.concatenate(

time: 159 us -> 191 us (1.20)
  waiting for transfers between devices: 16 us -> 69.2 us
  starting transfers between devices: 88.9 us -> 69.8 us
    reduce_scatter x0 -> x1, waiting for transfers between devices: none -> 47.1 us  [shards(): shared_sum = lax.psum_scatter(pair, CHIPS, scatter_dimension=0, tiled=True)]
    ppermute x8 -> x4, starting transfers between devices: 42 us -> 24.8 us  [swap(): return lax.ppermute(value, axis, [(0, 1), (1, 0)])]
    all_to_all x1, waiting for transfers between devices: 0.01 us -> 15.6 us  [shards(): lax.all_to_all(part.reshape(groups, capacity, half), 'expert', 0, 0, tile...]
    ppermute x8 -> x4, waiting for transfers between devices: 15.9 us -> 2.71 us  [swap(): return lax.ppermute(value, axis, [(0, 1), (1, 0)])]
    all_to_all x1, waiting for transfers between devices: 0.01 us -> 3.1 us  [shards(): lax.all_to_all(outbound.reshape(groups, capacity, half), 'expert', 0, 0,...]
    add x4 -> x0, other arithmetic: 2.28 us -> none  [the longest x1 1.2 us: shards(): pair = jnp.where(core == 0, left, right) + given.astype(F32)]
    all_to_all x1, starting transfers between devices: 6.33 us -> 4.21 us  [shards(): lax.all_to_all(part.reshape(groups, capacity, half), 'expert', 0, 0, tile...]
    convert_element_type x4 -> x1, other arithmetic: 0.1 us -> 2.02 us  [shards(): pair = pair.astype(BF16)]
  transfers between devices with their start and end apart: 13 -> 10, of which waited for: 5 -> 5; matrix products, arithmetic and copies ran while one was open for 20% -> 16% of each run, Pallas kernels for 0% -> 0%
where the time goes in v3:
time: 191 us; the launch traced here: 190 us
  starting transfers between devices  69.8 us (37%)
  waiting for transfers between devices  69.2 us (36%)
  matrix products  28.8 us (15%)
  between operations  13.7 us (7%)
  other arithmetic  5.05 us (3%)
  local copies, waits for them, and re-layouts  3.19 us (2%)
    reduce_scatter x1, waiting for transfers between devices, shards(): shared_sum = lax.psum_scatter(pair, CHIPS, scatter_dimension=0, tiled=True)  47.1 us
    dot_general x17, matrix products, dot(): return jnp.dot(a, b, preferred_element_type=F32)  26.6 us
    ppermute x4, starting transfers between devices, swap(): return lax.ppermute(value, axis, [(0, 1), (1, 0)])  24.8 us
    all_to_all x1, starting transfers between devices, shards(): lax.all_to_all(copies, CHIPS, 0, 0, tiled=True).reshape(half, rows)  19.4 us
    all_to_all x1, waiting for transfers between devices, shards(): lax.all_to_all(part.reshape(groups, capacity, half), 'expert', 0, 0, tile...  15.6 us
    all_to_all x1, starting transfers between devices, shards(): lax.all_to_all(routed_terms.reshape(chips, cores * own, half), CHIPS, 0,...  11.6 us
    all_to_all x1, starting transfers between devices, shards(): lax.all_to_all(outbound.reshape(groups, capacity, half), 'expert', 0, 0,...  9.79 us
    all_to_all x1, starting transfers between devices, shards(): lax.all_to_all(part.reshape(groups, capacity, half), 'expert', 0, 0, tile...  4.21 us
  transfers between devices with their start and end apart: 10, of which 5 were waited for; matrix products, arithmetic and copies ran while one was open for 16% of the time, Pallas kernels for 0%

profile of v3, /device:TPU:1, one launch (start us, length us, event | category | flops | bytes accessed | tf_op | source)
XLA Modules:
  0.0 189.8 jit_solution(5663507549841174645)
XLA Ops:
  6.5 1.8 pad.4
  8.4 1.4 convolution_convert_fusion.8
  10.5 19.4 %all-to-all-start = ((bf16[16,32,128]{2,1,0:T(8,128)(2,1)}), bf16[16,32,128]{2,1,0:T(8,128)(2,1)S(1)}, u32[]{:S(2)}, u32[]{:S(2)}) async-start(bf16[16,32,128]{2,1,0:T(8,128)(2,1)} %broadcast_in_dim.48), calls=%async_computation | async-start | bytes 262144 | tf_op jit(solution)/shard_map/all_to_all | solution.py:61
  30.4 2.7 %fusion.4 = f32[128,4096]{1,0:T(8,128)S(1)} fusion(bf16[84,4096]{1,0:T(8,128)(2,1)} %param.20, bf16[128,4096]{1,0:T(8,128)(2,1)S(1)} %copy-done, bf16[4096,84]{0,1:T(8,128)(2,1)} %param.19, f32[128,84]{0,1:T(8,128)S(1)} %fusion.28), kind=kOutput, calls=%fused_computation.20 | convolution fusion | flops 176225280 | bytes 4564992 | tf_op jit(solution)/shard_map/dot_general | solution.py:13
  33.2 0.9 select_convert_fusion
  34.0 2.8 %collective-permute-start = (bf16[128,2048]{1,0:T(8,128)(2,1)}, bf16[128,2048]{1,0:T(8,128)(2,1)}, u32[]{:S(2)}, u32[]{:S(2)}) collective-permute-start(bf16[128,2048]{1,0:T(8,128)(2,1)} %select_convert_fusion), channel_id=1, source_target_pairs={{0,1},{1,0},{2,3},{3,2},{4,5},{5,4},{6,7},{7,6},{8,9},{9,8},{10,11... | collective-permute-start | bytes 1572872 | tf_op jit(solution)/shard_map/ppermute | solution.py:17
  37.5 3.2 %convolution_convert_fusion.7 = bf16[512,336]{0,1:T(8,128)(2,1)} fusion(bf16[1,1024,336]{1,2,0:T(8,128)(2,1)} %param.15, s32[]{:T(128)S(6)} %mul.58, s32[512]{0:T(512)S(1)} %get-tuple-element.44, s32[512]{0:T(512)S(1)} %get-tuple-element.45, s32[512]{0:T(512)S(1)} %get-tuple-element.43, s32[512]{0:T(512)S(1)} %get-tuple-element.46, ...), kind=kOutput, calls=%fused_computation.14 | convolution fusion | flops 355639296 | bytes 1041412 | tf_op jit(solution)/shard_map/dot_general | solution.py:13
  40.7 1.9 %convolution_convert_fusion.6 = bf16[512,336]{0,1:T(8,128)(2,1)} fusion(bf16[1,1024,336]{1,2,0:T(8,128)(2,1)S(1)} %copy-done.5, s32[]{:T(128)S(6)} %mul.59, s32[512]{0:T(512)S(1)} %get-tuple-element.44, s32[512]{0:T(512)S(1)} %get-tuple-element.45, s32[512]{0:T(512)S(1)} %get-tuple-element.43, s32[512]{0:T(512)S(1)} %get-tuple-element.46, ...), kind=kOutput, calls=%fused_computation.13 | convolution fusion | flops 355639296 | bytes 1041412 | tf_op jit(solution)/shard_map/dot_general | solution.py:13
  42.6 1.1 convolution_convert_fusion.1
  43.7 9.8 %all-to-all-start.1 = ((bf16[32,16,512]{2,1,0:T(8,128)(2,1)}), bf16[32,16,512]{2,1,0:T(8,128)(2,1)}, u32[]{:S(2)}, u32[]{:S(2)}) async-start(bf16[32,16,512]{2,1,0:T(8,128)(2,1)} %bitcast.72), calls=%async_computation.1 | async-start | bytes 1048576 | tf_op jit(solution)/shard_map/all_to_all | solution.py:94
  53.5 3.1 %convolution_convert_fusion.5 = bf16[512,336]{0,1:T(8,128)(2,1)} fusion(bf16[1,1024,336]{1,2,0:T(8,128)(2,1)} %param.16, s32[]{:T(128)S(6)} %mul.58, s32[512]{0:T(512)S(1)} %get-tuple-element.44, s32[512]{0:T(512)S(1)} %get-tuple-element.45, s32[512]{0:T(512)S(1)} %get-tuple-element.43, s32[512]{0:T(512)S(1)} %get-tuple-element.46, ...), kind=kOutput, calls=%fused_computation.12 | convolution fusion | flops 355639296 | bytes 1041412 | tf_op jit(solution)/shard_map/dot_general | solution.py:13
  56.6 1.9 %convolution_convert_fusion.4 = bf16[512,336]{0,1:T(8,128)(2,1)} fusion(bf16[1,1024,336]{1,2,0:T(8,128)(2,1)S(1)} %copy-done.6, s32[]{:T(128)S(6)} %mul.59, s32[512]{0:T(512)S(1)} %get-tuple-element.44, s32[512]{0:T(512)S(1)} %get-tuple-element.45, s32[512]{0:T(512)S(1)} %get-tuple-element.43, s32[512]{0:T(512)S(1)} %get-tuple-element.46, ...), kind=kOutput, calls=%fused_computation.11 | convolution fusion | flops 355639296 | bytes 1041412 | tf_op jit(solution)/shard_map/dot_general | solution.py:13
  58.5 1.3 convolution_convert_fusion.3
  59.8 2.0 %convolution_convert_fusion.2 = bf16[336,512]{1,0:T(8,128)(2,1)} fusion(bf16[1,336,1024]{2,1,0:T(8,128)(2,1)S(1)} %copy-done.7, s32[]{:T(128)S(6)} %mul.59, s32[512]{0:T(512)S(1)} %get-tuple-element.44, s32[512]{0:T(512)S(1)} %get-tuple-element.45, s32[512]{0:T(512)S(1)} %get-tuple-element.43, s32[512]{0:T(512)S(1)} %get-tuple-element.46, ...), kind=kOutput, calls=%fused_computation.9 | convolution fusion | flops 355639296 | bytes 1041412 | tf_op jit(solution)/shard_map/dot_general | solution.py:13
  61.8 2.0 %add_convert_fusion.1 = bf16[128,2048]{1,0:T(8,128)(2,1)} fusion(bf16[128,2048]{1,0:T(8,128)(2,1)} %collective-permute-done, f32[128,4096]{1,0:T(8,128)S(1)} %fusion.4, pred[]{:T(512)S(6)} %eq.61), kind=kLoop, calls=%fused_computation.24 | loop fusion | flops 1048576 | bytes 3145729 | tf_op jit(solution)/shard_map/convert_element_type | solution.py:107
  63.8 3.1 %all-to-all-done.1 = bf16[32,16,512]{2,1,0:T(8,128)(2,1)} async-done(((bf16[32,16,512]{2,1,0:T(8,128)(2,1)}), bf16[32,16,512]{2,1,0:T(8,128)(2,1)}, u32[]{:S(2)}, u32[]{:S(2)}) %all-to-all-start.1) | async-done | bytes 524320 | tf_op jit(solution)/shard_map/all_to_all | solution.py:94
  66.9 7.4 %collective-permute-start.1 = (bf16[512,512]{1,0:T(8,128)(2,1)}, bf16[512,512]{1,0:T(8,128)(2,1)S(1)}, u32[]{:S(2)}, u32[]{:S(2)}) collective-permute-start(bf16[512,512]{1,0:T(8,128)(2,1)} %bitcast.5), channel_id=1, source_target_pairs={{0,1},{1,0},{2,3},{3,2},{4,5},{5,4},{6,7},{7,6},{8,9},{9,8},{10,11... | collective-permute-start | bytes 1572872 | tf_op jit(solution)/shard_map/ppermute | solution.py:17
  74.4 1.5 fusion.29
  75.9 1.6 fusion.30
  79.3 1.9 %collective-permute-start.2 = (bf16[512,512]{1,0:T(8,128)(2,1)S(1)}, bf16[512,512]{1,0:T(8,128)(2,1)S(1)}, u32[]{:S(2)}, u32[]{:S(2)}) collective-permute-start(bf16[512,512]{1,0:T(8,128)(2,1)S(1)} %convolution_convert_fusion), channel_id=1, source_target_pairs={{0,1},{1,0},{2,3},{3,2},{4,5},{5,4},{6,7},{7,6},{8,9},{9,8},{10,11... | collective-permute-start | bytes 1572872 | tf_op jit(solution)/shard_map/ppermute | solution.py:17
  81.3 1.9 collective-permute-done.2
  83.1 1.3 add_convert_fusion
  84.4 4.2 %all-to-all-start.2 = ((bf16[32,16,512]{2,1,0:T(8,128)(2,1)}), bf16[32,16,512]{2,1,0:T(8,128)(2,1)S(1)}, u32[]{:S(2)}, u32[]{:S(2)}) async-start(bf16[32,16,512]{2,1,0:T(8,128)(2,1)} %bitcast.8), calls=%async_computation.2 | async-start | bytes 1048576 | tf_op jit(solution)/shard_map/all_to_all | solution.py:119
  88.7 0.7 reduce-scatter.2.cloned.1.call-update
  89.8 15.6 %all-to-all-done.2 = bf16[32,16,512]{2,1,0:T(8,128)(2,1)S(1)} async-done(((bf16[32,16,512]{2,1,0:T(8,128)(2,1)}), bf16[32,16,512]{2,1,0:T(8,128)(2,1)S(1)}, u32[]{:S(2)}, u32[]{:S(2)}) %all-to-all-start.2) | async-done | bytes 524320 | tf_op jit(solution)/shard_map/all_to_all | solution.py:119
  105.6 0.9 fusion.2
  106.5 11.6 %all-to-all-start.3 = ((bf16[16,8,512]{2,1,0:T(8,128)(2,1)}), bf16[16,8,512]{2,1,0:T(8,128)(2,1)S(1)}, u32[]{:S(2)}, u32[]{:S(2)}) async-start(bf16[16,8,512]{2,1,0:T(8,128)(2,1)} %fusion.2), calls=%async_computation.3 | async-start | bytes 262144 | tf_op jit(solution)/shard_map/all_to_all | solution.py:138
  118.1 47.1 %reduce-scatter.2.cloned.1.call-done = bf16[8,2048]{1,0:T(8,128)(2,1)} async-done(((bf16[128,2048]{1,0:T(8,128)(2,1)}), bf16[8,2048]{1,0:T(8,128)(2,1)}) %reduce-scatter.2.cloned.1.call-update) | async-done | bytes 32784 | tf_op jit(solution)/shard_map/reduce_scatter | solution.py:109
  165.2 0.8 convert_select_fusion.1
  166.1 2.8 %convolution_add_fusion = f32[8,4096]{1,0:T(8,128)S(1)} fusion(bf16[8,512]{1,0:T(8,128)(2,1)S(1)} %reduce_sum.35, bf16[512,4608]{1,0:T(8,128)(2,1)} %all-gather.2.cloned.1.call-done, f32[8,2048]{1,0:T(8,128)S(1)} %get-tuple-element.42, f32[8,2048]{1,0:T(8,128)S(1)} %get-tuple-element.41), kind=kOutput, calls=%fused_computation | convolution fusion | flops 33619968 | bytes 4464640 | tf_op jit(solution)/shard_map/dot_general | solution.py:13
  168.9 12.6 %collective-permute-start.3 = (bf16[4,4096]{1,0:T(4,128)(2,1)S(1)}, bf16[4,4096]{1,0:T(4,128)(2,1)S(1)}, u32[]{:S(2)}, u32[]{:S(2)}) collective-permute-start(bf16[4,4096]{1,0:T(4,128)(2,1)S(1)} %select_convert_fusion.1), channel_id=1, source_target_pairs={{0,1},{1,0},{2,3},{3,2},{4,5},{5,4},{6,7},{7,6},{8,9},{9,8},{10,11... | collective-permute-start | bytes 98312 | tf_op jit(solution)/shard_map/ppermute | solution.py:17
  181.5 0.8 collective-permute-done.3
  (49 shorter events, 4.9 us)
Async XLA Ops:
  6.5 1.9 copy-start
  6.5 23.4 %copy-start.1 = (bf16[4096,84]{0,1:T(8,128)(2,1)S(1)}, bf16[4096,84]{0,1:T(8,128)(2,1)}, u32[]{:S(2)}) copy-start(bf16[4096,84]{0,1:T(8,128)(2,1)} %param.18) | copy-start | bytes 2064388
  6.5 98.8 %all-gather.2.cloned.1.call-start = ((), (), s32[]{:S(2)}) async-start(), calls=%async_computation.5 | async-start | bytes 5013504 | tf_op jit(solution)/shard_map/all_gather | solution.py:55
  10.5 32.1 %all-to-all-start = ((bf16[16,32,128]{2,1,0:T(8,128)(2,1)}), bf16[16,32,128]{2,1,0:T(8,128)(2,1)S(1)}, u32[]{:S(2)}, u32[]{:S(2)}) async-start(bf16[16,32,128]{2,1,0:T(8,128)(2,1)} %broadcast_in_dim.48), calls=%async_computation | async-start | bytes 262144 | tf_op jit(solution)/shard_map/all_to_all | solution.py:61
  30.4 6.6 %copy-start.3 = (s32[128,22]{0,1:T(8,128)S(1)}, s32[128,22]{0,1:T(8,128)}, u32[]{:S(2)}) copy-start(s32[128,22]{0,1:T(8,128)} %param.13) | copy-start | bytes 33796
  34.0 27.8 %collective-permute-start = (bf16[128,2048]{1,0:T(8,128)(2,1)}, bf16[128,2048]{1,0:T(8,128)(2,1)}, u32[]{:S(2)}, u32[]{:S(2)}) collective-permute-start(bf16[128,2048]{1,0:T(8,128)(2,1)} %select_convert_fusion), channel_id=1, source_target_pairs={{0,1},{1,0},{2,3},{3,2},{4,5},{5,4},{6,7},{7,6},{8,9},{9,8},{10,11... | collective-permute-start | bytes 1572872 | tf_op jit(solution)/shard_map/ppermute | solution.py:17
  37.5 3.2 %copy-start.5 = (bf16[1,1024,336]{1,2,0:T(8,128)(2,1)S(1)}, bf16[1,1024,336]{1,2,0:T(8,128)(2,1)}, u32[]{:S(2)}) copy-start(bf16[1,1024,336]{1,2,0:T(8,128)(2,1)} %param.15) | copy-start | bytes 2064388
  43.7 23.2 %all-to-all-start.1 = ((bf16[32,16,512]{2,1,0:T(8,128)(2,1)}), bf16[32,16,512]{2,1,0:T(8,128)(2,1)}, u32[]{:S(2)}, u32[]{:S(2)}) async-start(bf16[32,16,512]{2,1,0:T(8,128)(2,1)} %bitcast.72), calls=%async_computation.1 | async-start | bytes 1048576 | tf_op jit(solution)/shard_map/all_to_all | solution.py:94
  53.5 3.1 %copy-start.6 = (bf16[1,1024,336]{1,2,0:T(8,128)(2,1)S(1)}, bf16[1,1024,336]{1,2,0:T(8,128)(2,1)}, u32[]{:S(2)}) copy-start(bf16[1,1024,336]{1,2,0:T(8,128)(2,1)} %param.16) | copy-start | bytes 2064388
  56.6 1.9 %copy-start.7 = (bf16[1,336,1024]{2,1,0:T(8,128)(2,1)S(1)}, bf16[1,336,1024]{2,1,0:T(8,128)(2,1)}, u32[]{:S(2)}) copy-start(bf16[1,336,1024]{2,1,0:T(8,128)(2,1)} %param.17) | copy-start | bytes 2064388
  63.8 13.6 %copy-start.2 = (bf16[512,336]{0,1:T(8,128)(2,1)S(1)}, bf16[512,336]{0,1:T(8,128)(2,1)}, u32[]{:S(2)}) copy-start(bf16[512,336]{0,1:T(8,128)(2,1)} %convolution_convert_fusion.6) | copy-start | bytes 1032196
  66.9 10.5 %collective-permute-start.1 = (bf16[512,512]{1,0:T(8,128)(2,1)}, bf16[512,512]{1,0:T(8,128)(2,1)S(1)}, u32[]{:S(2)}, u32[]{:S(2)}) collective-permute-start(bf16[512,512]{1,0:T(8,128)(2,1)} %bitcast.5), channel_id=1, source_target_pairs={{0,1},{1,0},{2,3},{3,2},{4,5},{5,4},{6,7},{7,6},{8,9},{9,8},{10,11... | collective-permute-start | bytes 1572872 | tf_op jit(solution)/shard_map/ppermute | solution.py:17
  75.9 2.0 %copy-start.9 = (bf16[512,336]{0,1:T(8,128)(2,1)S(1)}, bf16[512,336]{0,1:T(8,128)(2,1)}, u32[]{:S(2)}) copy-start(bf16[512,336]{0,1:T(8,128)(2,1)} %convolution_convert_fusion.4) | copy-start | bytes 1032196
  77.9 1.0 copy-start.8
  78.8 10.5 %copy-start.4 = (f32[128,22]{0,1:T(8,128)S(1)}, f32[128,22]{0,1:T(8,128)}, u32[]{:S(2)}) copy-start(f32[128,22]{0,1:T(8,128)} %param.14) | copy-start | bytes 33796
  79.3 3.8 %collective-permute-start.2 = (bf16[512,512]{1,0:T(8,128)(2,1)S(1)}, bf16[512,512]{1,0:T(8,128)(2,1)S(1)}, u32[]{:S(2)}, u32[]{:S(2)}) collective-permute-start(bf16[512,512]{1,0:T(8,128)(2,1)S(1)} %convolution_convert_fusion), channel_id=1, source_target_pairs={{0,1},{1,0},{2,3},{3,2},{4,5},{5,4},{6,7},{7,6},{8,9},{9,8},{10,11... | collective-permute-start | bytes 1572872 | tf_op jit(solution)/shard_map/ppermute | solution.py:17
  84.4 21.0 %all-to-all-start.2 = ((bf16[32,16,512]{2,1,0:T(8,128)(2,1)}), bf16[32,16,512]{2,1,0:T(8,128)(2,1)S(1)}, u32[]{:S(2)}, u32[]{:S(2)}) async-start(bf16[32,16,512]{2,1,0:T(8,128)(2,1)} %bitcast.8), calls=%async_computation.2 | async-start | bytes 1048576 | tf_op jit(solution)/shard_map/all_to_all | solution.py:119
  88.6 76.6 %reduce-scatter.2.cloned.1.call-start = ((), (), s32[]{:S(2)}) async-start(), calls=%async_computation.6 | async-start | bytes 557056 | tf_op jit(solution)/shard_map/reduce_scatter | solution.py:109
  106.5 59.5 %all-to-all-start.3 = ((bf16[16,8,512]{2,1,0:T(8,128)(2,1)}), bf16[16,8,512]{2,1,0:T(8,128)(2,1)S(1)}, u32[]{:S(2)}, u32[]{:S(2)}) async-start(bf16[16,8,512]{2,1,0:T(8,128)(2,1)} %fusion.2), calls=%async_computation.3 | async-start | bytes 262144 | tf_op jit(solution)/shard_map/all_to_all | solution.py:138
  168.9 13.4 %collective-permute-start.3 = (bf16[4,4096]{1,0:T(4,128)(2,1)S(1)}, bf16[4,4096]{1,0:T(4,128)(2,1)S(1)}, u32[]{:S(2)}, u32[]{:S(2)}) collective-permute-start(bf16[4,4096]{1,0:T(4,128)(2,1)S(1)} %select_convert_fusion.1), channel_id=1, source_target_pairs={{0,1},{1,0},{2,3},{3,2},{4,5},{5,4},{6,7},{7,6},{8,9},{9,8},{10,11... | collective-permute-start | bytes 98312 | tf_op jit(solution)/shard_map/ppermute | solution.py:17
Sparse Core Ops, SparseCore 0:
  10.0 85.0 all-gather.1
  98.5 66.6 reduce-scatter.1
